TPU v7x, 32 devices: a whole 2x2x4 slice. The times are simulated.
32 devices in a mesh: row: 4 (over x, core), col: 8 (over z, y).
Axes of the slice: x: 2, y: 2, z: 4, core: 2. Of those that a mesh axis runs over, the one named last changes fastest.
Arguments:
- lambda_amps: float32 [256, 32768], P('row', 'col'), may hold values from -6 to 6
- integrals: float32 [32768, 16384], P('col', 'row'), may hold values from -0.046875 to 0.046875
- symmetry_map: int32 [256, 128], P('col', 'row'), may hold values 0 or 1
- base_residual: float32 [256, 16384], P('col', 'row'), may hold values from -6 to 6
Outputs:
- residual: float32 [256, 16384], P('col', 'row')
All inputs are finite; a program needn't handle non-finite values. No bound on the sum of `symmetry_map` on one device may be relied on, other than what follows from the above.
Results may differ from a plain program's by a relative error of at most 0.0001.
Values sent between devices are 32-bit elements; how exact they have to be, the bound alone decides.
No kernel may reach another device: no remote copies, remote signals or barrier semaphores. Data moves between devices by JAX's collectives and lax.ppermute only.
A program may use at most 192 MiB of HBM per device.

v0:
```python
import jax
import jax.numpy as jnp
from jax import lax
from jax.sharding import PartitionSpec as P

TILE = 128


def body(lambda_amps, integrals, symmetry_map, base_residual):
    kdev, ndev = integrals.shape
    tile_size = TILE
    flags = symmetry_map.astype(jnp.float32)
    masked = (
        integrals.reshape(kdev // tile_size, tile_size, ndev // tile_size, tile_size)
        * flags[:, None, :, None]
    ).reshape(kdev, ndev)
    partial_sums = jnp.dot(
        lax.all_gather(lambda_amps, "row", axis=0, tiled=True),
        masked,
        preferred_element_type=jnp.float32,
        precision=lax.Precision.HIGHEST,
    )
    ladder = lax.psum_scatter(partial_sums, "col", scatter_dimension=0, tiled=True)
    return base_residual + ladder


def solution(mesh):
    placed = (P("row", "col"), P("col", "row"), P("col", "row"), P("col", "row"))
    return jax.shard_map(
        body, mesh=mesh, in_specs=placed, out_specs=P("col", "row"), check_vma=False
    )
```

profile of v0, /device:TPU:2, one launch (start us, length us, event | category | flops | bytes accessed | tf_op | source)
XLA Modules:
  0.0 290.2 jit_solution(6293131558862769389)
XLA Ops:
  6.5 0.0 all-gather.2.cloned.1.call-start
  6.5 0.7 all-gather.2.cloned.1.call-update
  7.3 0.0 reduce-scatter.4.cloned.1.call-start
  7.3 0.7 convert_element_type.3
  8.0 35.5 %all-gather.2.cloned.1.call-done = f32[256,4096]{1,0:T(8,128)} async-done(((f32[64,4096]{1,0:T(8,128)}), f32[256,4096]{1,0:T(8,128)}) %all-gather.2.cloned.1.call-update) | async-done | bytes 4194320 | tf_op jit(solution)/shard_map/all_gather | solution.py:18
  43.5 0.0 copy-start
  43.5 21.8 %mul.11 = f32[32,128,32,128]{3,2,1,0:T(8,128)} broadcast(f32[32,32]{1,0:T(8,128)S(1)} %convert_element_type.3), dimensions={0,2} | broadcast | bytes 67112960 | tf_op jit(solution)/shard_map/mul | solution.py:14
  65.3 0.0 copy-done
  65.3 0.0 copy-start.1
  65.3 121.3 %fusion.2 = f32[256,4096]{0,1:T(8,128)} fusion(f32[256,4096]{1,0:T(8,128)S(1)} %copy-done, f32[4096,4096]{1,0:T(8,128)} %param.5, f32[512,8,32,128]{3,2,1,0:T(8,128)} %bitcast.3), kind=kOutput, calls=%fused_computation.3 | convolution fusion | flops 51556384768 | bytes 142606336 | tf_op jit(solution)/shard_map/dot_general | solution.py:17
  186.6 5.6 %copy.10 = f32[256,4096]{1,0:T(8,128)} copy(f32[256,4096]{0,1:T(8,128)} %fusion.2) | data formatting | bytes 8388608
  192.2 0.0 reduce-scatter.4.cloned.1.call-update
  192.3 89.2 %reduce-scatter.4.cloned.1.call-done = f32[32,4096]{1,0:T(8,128)} async-done(((f32[256,4096]{1,0:T(8,128)}), f32[32,4096]{1,0:T(8,128)}) %reduce-scatter.4.cloned.1.call-update) | async-done | bytes 524304 | tf_op jit(solution)/shard_map/reduce_scatter | solution.py:23
  281.5 0.0 copy-done.1
  281.5 1.9 add.5
Async XLA Ops:
  6.5 37.0 %all-gather.2.cloned.1.call-start = ((), (), s32[]{:S(2)}) async-start(), calls=%async_computation.1 | async-start | bytes 5242880 | tf_op jit(solution)/shard_map/all_gather | solution.py:18
  7.3 274.2 %reduce-scatter.4.cloned.1.call-start = ((), (), s32[]{:S(2)}) async-start(), calls=%async_computation.2 | async-start | bytes 4718592 | tf_op jit(solution)/shard_map/reduce_scatter | solution.py:23
  43.5 21.8 %copy-start = (f32[256,4096]{1,0:T(8,128)S(1)}, f32[256,4096]{1,0:T(8,128)}, u32[]{:S(2)}) copy-start(f32[256,4096]{1,0:T(8,128)} %all-gather.2.cloned.1.call-done) | copy-start | bytes 12582916
  65.3 216.2 %copy-start.1 = (f32[32,4096]{1,0:T(8,128)S(1)}, f32[32,4096]{1,0:T(8,128)}, u32[]{:S(2)}) copy-start(f32[32,4096]{1,0:T(8,128)} %param.7) | copy-start | bytes 1572868
Sparse Core Ops, SparseCore 0:
  8.9 34.5 all-gather.1
  192.4 89.0 reduce-scatter.3
where the time goes:
time: 292 us; the launch traced here: 290 us
  waiting for transfers between devices  125 us (43%)
  matrix products  121 us (41%)
  local copies, waits for them, and re-layouts  27.4 us (9%)
  between operations  13.4 us (5%)
    dot_general x1, matrix products, body(): jnp.dot(lax.all_gather(lambda_amps, 'row', axis=0, tiled=True), masked, p...  121 us
    reduce_scatter x1, waiting for transfers between devices, body(): lax.psum_scatter(partial_sums, 'col', scatter_dimension=0, tiled=True)  89.2 us
    all_gather x1, waiting for transfers between devices, body(): lax.all_gather(lambda_amps, 'row', axis=0, tiled=True)  35.5 us
    mul x1, local copies, waits for them, and re-layouts, body(): integrals.reshape(kdev // tile_size, tile_size, ndev // tile_size, tile_s...  21.8 us
  transfers between devices with their start and end apart: 2, of which 2 were waited for; matrix products, arithmetic and copies ran while one was open for 0% of the time, Pallas kernels for 0%

commit v1 on v0

v1 whole, which is shorter than its diff:
```python
import functools

import jax
import jax.numpy as jnp
from jax import lax
from jax.experimental import pallas as pl
from jax.experimental.pallas import tpu as pltpu
from jax.sharding import PartitionSpec as P

TILE = 128
WIDE = 2 * TILE
F32, BF16 = jnp.float32, jnp.bfloat16
GROUP = 4
DEPTH = 3
VMEM = pl.BlockSpec(memory_space=pltpu.VMEM)
SMEM = pl.BlockSpec(memory_space=pltpu.SMEM)


def block_lists(flags):
    kb, nb = flags.shape
    on = (flags != 0).reshape(kb, nb // 2, 2).astype(jnp.int32)
    either = on[..., 0] | on[..., 1]
    place = jnp.arange(kb, dtype=jnp.int32)
    code = place[:, None] * 4 + on[..., 0] + 2 * on[..., 1]
    lower = (place[:, None] > place[None, :]).astype(jnp.int32)
    rank = jnp.sum(lower[:, :, None] * either[None], axis=1)
    hit = (rank[None] == place[:, None, None]) & (either[None] != 0)
    listed = jnp.sum(jnp.where(hit, code[None], 0), axis=1)
    count = jnp.sum(either, axis=0)
    listed = jnp.where(place[:, None] < count[None], listed, kb * 4)
    return listed.T.reshape(-1), (count + GROUP - 1) // GROUP


def split_rows(o_ref, first, x):
    rows, half = x.shape[0], o_ref.shape[1] // 2
    for p in range(x.shape[1] // TILE):
        part = x[:, p * TILE : (p + 1) * TILE]
        high = part.astype(BF16)
        o_ref[p, first : first + rows] = high
        o_ref[p, half + first : half + first + rows] = (part - high.astype(F32)).astype(BF16)


def order_kernel(at_ref, own_ref, mate_ref, o_ref):
    y, z1, core = at_ref[0], at_ref[1], at_ref[2]
    o_ref[o_ref.shape[0] - 1] = jnp.zeros(o_ref.shape[1:], BF16)
    part = own_ref.shape[0] // 2
    for j in range(4):
        row = y if j >= 2 else 1 - y
        side = z1 if j % 2 else 1 - z1
        rows = pl.ds(pl.multiple_of(row * part, part), part)

        @pl.when(side == core)
        def _():
            split_rows(o_ref, j * part, own_ref[rows])

        @pl.when(side != core)
        def _():
            split_rows(o_ref, j * part, mate_ref[rows])


def ordered(at, own, mate):
    m, k = own.shape
    return pl.pallas_call(
        order_kernel,
        out_shape=jax.ShapeDtypeStruct((k // TILE + 1, 4 * m, TILE), BF16),
        in_specs=[SMEM, VMEM, VMEM],
        out_specs=VMEM,
        compiler_params=pltpu.CompilerParams(vmem_limit_bytes=24 * 2**20),
        cost_estimate=pl.CostEstimate(flops=8 * m * k, bytes_accessed=16 * m * k, transcendentals=0),
    )(at, own, mate)


def plain_kernel(l_ref, o_ref):
    o_ref[o_ref.shape[0] - 1] = jnp.zeros(o_ref.shape[1:], BF16)
    split_rows(o_ref, 0, l_ref[...])


def plain(lam):
    m, k = lam.shape
    return pl.pallas_call(
        plain_kernel,
        out_shape=jax.ShapeDtypeStruct((k // TILE + 1, 2 * m, TILE), BF16),
        in_specs=[VMEM],
        out_specs=VMEM,
        compiler_params=pltpu.CompilerParams(vmem_limit_bytes=24 * 2**20),
    )(lam)


def ladder_kernel(first, pairs, kb, list_ref, count_ref, l_ref, g_ref, send_ref, keep_ref, buf, sem):
    m = l_ref.shape[1] // 2

    def start(q, slot):
        def some(c, _):
            for u in range(GROUP):
                p = lax.shift_right_logical(list_ref[q * kb + c * GROUP + u], 2)
                p = jnp.where(p == kb, 0, p)
                pltpu.make_async_copy(
                    g_ref.at[pl.ds(pl.multiple_of(p * TILE, TILE), TILE), pl.ds(pl.multiple_of(q * WIDE, WIDE), WIDE)],
                    buf.at[slot, pl.ds(pl.multiple_of((c * GROUP + u) * TILE, TILE), TILE)],
                    sem.at[slot],
                ).start()
            return 0

        lax.fori_loop(0, count_ref[q], some, 0)

    def wait(q, slot):
        def some(c, _):
            rows = pl.ds(0, GROUP * TILE)
            pltpu.make_async_copy(g_ref.at[rows, pl.ds(0, WIDE)], buf.at[slot, rows], sem.at[slot]).wait()
            return 0

        lax.fori_loop(0, count_ref[q], some, 0)

    for d in range(min(DEPTH - 1, pairs)):
        start(first + d, d)

    def step(i, _):
        q, slot, ahead = first + i, lax.rem(i, DEPTH), i + DEPTH - 1

        @pl.when(ahead < pairs)
        def _():
            start(first + ahead, lax.rem(ahead, DEPTH))

        wait(q, slot)
        columns = pl.ds(pl.multiple_of(i * WIDE, WIDE), WIDE)
        count = count_ref[q]
        for c in range(kb // GROUP + 1):

            @pl.when(count == c)
            def _():
                both, low = jnp.zeros((2 * m, WIDE), F32), jnp.zeros((m, WIDE), F32)
                for k in range(0, c * GROUP, 2):
                    lefts, rights = [], []
                    for u in (k, k + 1):
                        code = list_ref[q * kb + u]
                        lefts.append(l_ref[lax.shift_right_logical(code, 2)])
                        rows = pl.ds(u * TILE, TILE)
                        rights.append(
                            jnp.concatenate(
                                [
                                    buf[slot, rows, 0:TILE] * (code & 1).astype(F32),
                                    buf[slot, rows, TILE:WIDE] * (lax.shift_right_logical(code, 1) & 1).astype(F32),
                                ],
                                axis=1,
                            )
                        )
                    left, right = jnp.concatenate(lefts, axis=1), jnp.concatenate(rights, axis=0)
                    high = right.astype(BF16)
                    rest = (right - high.astype(F32)).astype(BF16)
                    both = both + jnp.dot(left, high, preferred_element_type=F32)
                    low = low + jnp.dot(left[:m], rest, preferred_element_type=F32)
                total = both[:m] + (both[m:] + low)
                send_ref[:, columns] = total[: m // 2]
                keep_ref[:, columns] = total[m // 2 :]

        return 0

    lax.fori_loop(0, pairs, step, 0)


def ladder(lists, left, integrals, first, pairs):
    kb, m = left.shape[0] - 1, left.shape[1] // 2
    out = jax.ShapeDtypeStruct((m // 2, pairs * WIDE), F32)
    return pl.pallas_call(
        functools.partial(ladder_kernel, first, pairs, kb),
        out_shape=[out, out],
        in_specs=[SMEM, SMEM, VMEM, pl.BlockSpec(memory_space=pl.ANY)],
        out_specs=[VMEM, VMEM],
        scratch_shapes=[pltpu.VMEM((DEPTH, kb * TILE, WIDE), F32), pltpu.SemaphoreType.DMA((DEPTH,))],
        compiler_params=pltpu.CompilerParams(vmem_limit_bytes=32 * 2**20),
        cost_estimate=pl.CostEstimate(
            flops=24 * m * kb * TILE * pairs * WIDE, bytes_accessed=4 * kb * TILE * pairs * WIDE, transcendentals=0
        ),
    )(*lists, left, integrals)


def body_any(lambda_amps, integrals, symmetry_map, base_residual):
    lists = block_lists(symmetry_map)
    gathered = lax.all_gather(lambda_amps, "row", axis=0, tiled=True)
    pairs = integrals.shape[1] // WIDE
    sums = []
    for first in range(0, gathered.shape[0], TILE):
        sums += ladder(lists, plain(gathered[first : first + TILE]), integrals, 0, pairs)
    return base_residual + lax.psum_scatter(jnp.concatenate(sums), "col", scatter_dimension=0, tiled=True)


NEAR = (7, 7, 2)
FAR = (8, 5, 3)


def body_cube(rows, cols, lambda_amps, integrals, symmetry_map, base_residual):
    row, col = lax.axis_index("row"), lax.axis_index("col")
    x, core = row // 2, row % 2
    y, z1, z2 = col % 2, col // 2 % 2, col // 4
    at = jnp.stack([y, z1, core]).astype(jnp.int32)

    def swap(array, axis, step):
        n = rows if axis == "row" else cols
        return lax.ppermute(array, axis, [(i, i ^ step) for i in range(n)])

    def across(array, near):
        hops = []
        for r in range(rows):
            for c in range(cols):
                if (r // 2 != c // 4) == near:
                    hops.append((r * cols + c, r * cols + (c ^ 4)))
        return lax.ppermute(array, ("row", "col"), hops)

    def after(array, *earlier):
        return lax.optimization_barrier((array, *earlier))[0]

    far = swap(lambda_amps, "row", 2)
    mate = swap(lambda_amps, "row", 1)
    lists = block_lists(symmetry_map)
    part = lambda_amps.shape[0] // 2
    cuts = [(True, pairs) for pairs in NEAR] + [(False, pairs) for pairs in FAR]
    left = ordered(at, lambda_amps, mate)
    y_sent, z1_sent, z2_sent, done, fresh = [], [], [], [], []
    first = 0

    def finish_y(i, *earlier):
        keep, there = y_sent[i]
        total = keep + after(there, *earlier)
        z1_sent.append((total[part:], swap(total[:part], "col", 2)))
        fresh.append(total)

    def finish_z1(i, *earlier):
        keep, there = z1_sent[i]
        total = keep + after(there, *earlier)
        z2_sent.append((total, across(total, cuts[i][0])))
        fresh.append(total)

    def finish_z2(i, *earlier):
        keep, there = z2_sent[i]
        done.append(keep + after(there, *earlier))
        fresh.append(done[-1])

    for step, (near, pairs) in enumerate(cuts):
        if step == len(NEAR) - 1:
            far = after(far, fresh[-1])
            far_mate = swap(far, "row", 1)
        if step == len(NEAR):
            first = 0
            left = ordered(at, far, after(far_mate, fresh[-1]))
        if step > 0:
            left = after(left, *fresh)
            fresh.clear()
        send, keep = ladder(lists, left, integrals, first, pairs)
        first += pairs
        fresh.append(keep)
        y_sent.append((keep, swap(send, "col", 1)))
        if step >= 3:
            finish_z2(step - 3, keep)
        if step >= 2:
            finish_z1(step - 2, keep)
        if step >= 1:
            finish_y(step - 1, keep)
    last = len(cuts) - 1
    finish_z1(last - 1)
    finish_y(last)
    finish_z1(last)
    for i in range(last - 2, last + 1):
        finish_z2(i)
    near_sum = jnp.concatenate(done[: len(NEAR)], axis=1)
    far_sum = jnp.concatenate(done[len(NEAR) :], axis=1)
    return base_residual + jnp.where(z2 == x, near_sum, far_sum)


def solution(mesh):
    placed = (P("row", "col"), P("col", "row"), P("col", "row"), P("col", "row"))
    rows, cols = mesh.shape["row"], mesh.shape["col"]
    body = functools.partial(body_cube, rows, cols) if (rows, cols) == (4, 8) else body_any
    return jax.shard_map(body, mesh=mesh, in_specs=placed, out_specs=P("col", "row"), check_vma=False)
```

time: 292 us -> 115 us (0.39)
  matrix products: 121 us -> 0 us
  waiting for transfers between devices: 125 us -> 23.9 us
  Pallas kernels: 0 us -> 53.2 us
  starting transfers between devices: 0.04 us -> 31.7 us
  local copies, waits for them, and re-layouts: 27.4 us -> 2.33 us
  between operations: 13.4 us -> 0.43 us
    dot_general x1 -> x0, matrix products: 121 us -> none  [body(): jnp.dot(lax.all_gather(lambda_amps, 'row', axis=0, tiled=True), masked, p...]
    reduce_scatter x1 -> x0, waiting for transfers between devices: 89.2 us -> none  [body(): lax.psum_scatter(partial_sums, 'col', scatter_dimension=0, tiled=True)]
    pallas_call x0 -> x8, Pallas kernels: none -> 53.2 us  [the longest x6 51.6 us: ladder(): pl.pallas_call(functools.partial(ladder_kernel, first, pairs, kb), out_sh...]
    all_gather x1 -> x0, waiting for transfers between devices: 35.5 us -> none  [body(): lax.all_gather(lambda_amps, 'row', axis=0, tiled=True)]
    ppermute x0 -> x21, starting transfers between devices: none -> 31.7 us  [the longest x6 16.7 us: across(): return lax.ppermute(array, ('row', 'col'), hops)]
    ppermute x0 -> x21, waiting for transfers between devices: none -> 23.9 us  [the longest x15 14.5 us: swap(): return lax.ppermute(array, axis, [(i, i ^ step) for i in range(n)])]
    mul x1 -> x0, local copies, waits for them, and re-layouts: 21.8 us -> none  [body(): integrals.reshape(kdev // tile_size, tile_size, ndev // tile_size, tile_s...]
    unnamed x5, local copies, waits for them, and re-layouts: 5.63 us -> 2.02 us
  transfers between devices with their start and end apart: 2 -> 21, of which waited for: 2 -> 8; matrix products, arithmetic and copies ran while one was open for 0% -> 3% of each run, Pallas kernels for 0% -> 46%
where the time goes in v1:
time: 115 us
  Pallas kernels  53.2 us (46%)
  starting transfers between devices  31.7 us (28%)
  waiting for transfers between devices  23.9 us (21%)
  other arithmetic  2.95 us (3%)
  local copies, waits for them, and re-layouts  2.33 us (2%)
    pallas_call x6, Pallas kernels, ladder(): pl.pallas_call(functools.partial(ladder_kernel, first, pairs, kb), out_sh...  51.6 us
    ppermute x6, starting transfers between devices, across(): return lax.ppermute(array, ('row', 'col'), hops)  16.7 us
    ppermute x15, starting transfers between devices, swap(): return lax.ppermute(array, axis, [(i, i ^ step) for i in range(n)])  15 us
    ppermute x15, waiting for transfers between devices, swap(): return lax.ppermute(array, axis, [(i, i ^ step) for i in range(n)])  14.5 us
    ppermute x6, waiting for transfers between devices, across(): return lax.ppermute(array, ('row', 'col'), hops)  9.37 us
  transfers between devices with their start and end apart: 21, of which 8 were waited for; matrix products, arithmetic and copies ran while one was open for 3% of the time, Pallas kernels for 46%

profile of v1, /device:TPU:2, one launch (start us, length us, event | category | flops | bytes accessed | tf_op | source)
XLA Modules:
  0.0 114.5 jit_solution(16969569651683465907)
XLA Ops:
  4.9 10.9 %shard_map.47 = (f32[64,1792]{1,0:T(8,128)S(1)}, f32[64,1792]{1,0:T(8,128)S(1)}) custom-call(s32[512]{0:T(512)S(1)} %reshape.66.list_ref, s32[16]{0:T(128)S(1)} %and_select_fusion.count_ref, bf16[33,256,128]{2,1,0:T(8,128)(2,1)S(1)} %shard_map.46.l_ref, f32[4096,4096]{1,0:T(8,128)} %g_ref.11), custom_call_target="tpu_custom_call" | custom-call | flops 22548578304 | bytes 29360128 | tf_op jit(solution)/shard_map/pallas_call | solution.py:164
  15.8 1.7 %collective-permute-start.1 = (f32[64,1792]{1,0:T(8,128)S(1)}, f32[64,1792]{1,0:T(8,128)S(1)}, u32[]{:S(2)}, u32[]{:S(2)}) collective-permute-start(f32[64,1792]{1,0:T(8,128)S(1)} %get-tuple-element.37), channel_id=1, source_target_pairs={{0,1},{1,0},{2,3},{3,2},{4,5},{5,4},{6,7},{7,6},{8,9},{9,8},{10,11... | collective-permute-start | bytes 1376264 | tf_op jit(solution)/shard_map/ppermute | solution.py:199
  17.5 10.6 %shard_map.48 = (f32[64,1792]{1,0:T(8,128)S(1)}, f32[64,1792]{1,0:T(8,128)S(1)}) custom-call(s32[512]{0:T(512)S(1)} %reshape.66.list_ref, s32[16]{0:T(128)S(1)} %and_select_fusion.count_ref, bf16[33,256,128]{2,1,0:T(8,128)(2,1)S(1)} %shard_map.46.l_ref, f32[4096,4096]{1,0:T(8,128)} %g_ref.11), custom_call_target="tpu_custom_call" | custom-call | flops 22548578304 | bytes 29360128 | tf_op jit(solution)/shard_map/pallas_call | solution.py:164
  28.6 2.5 %collective-permute-start.2 = (f32[32,1792]{1,0:T(8,128)S(1)}, f32[32,1792]{1,0:T(8,128)S(1)}, u32[]{:S(2)}, u32[]{:S(2)}) collective-permute-start(f32[32,1792]{1,0:T(8,128)S(1)} %slice.61), channel_id=1, source_target_pairs={{0,2},{1,3},{2,0},{3,1},{4,6},{5,7},{6,4},{7,5},{8,10},{9,11},{10,... | collective-permute-start | bytes 688136 | tf_op jit(solution)/shard_map/ppermute | solution.py:199
  31.1 4.4 %shard_map.49 = (f32[64,512]{1,0:T(8,128)S(1)}, f32[64,512]{1,0:T(8,128)S(1)}) custom-call(s32[512]{0:T(512)S(1)} %reshape.66.list_ref, s32[16]{0:T(128)S(1)} %and_select_fusion.count_ref, bf16[33,256,128]{2,1,0:T(8,128)(2,1)S(1)} %shard_map.46.l_ref, f32[4096,4096]{1,0:T(8,128)} %g_ref.11), custom_call_target="tpu_custom_call" | custom-call | flops 6442450944 | bytes 8388608 | tf_op jit(solution)/shard_map/pallas_call | solution.py:164
  35.6 4.4 %collective-permute-done.6 = f32[64,1792]{1,0:T(8,128)S(1)} collective-permute-done((f32[64,1792]{1,0:T(8,128)S(1)}, f32[64,1792]{1,0:T(8,128)S(1)}, u32[]{:S(2)}, u32[]{:S(2)}) %collective-permute-start.6) | collective-permute-done | bytes 458784 | tf_op jit(solution)/shard_map/ppermute | solution.py:199
  40.0 2.2 %collective-permute-start.7 = (f32[32,1792]{1,0:T(8,128)S(1)}, f32[32,1792]{1,0:T(8,128)S(1)}, u32[]{:S(2)}, u32[]{:S(2)}) collective-permute-start(f32[32,1792]{1,0:T(8,128)S(1)} %slice.63), channel_id=1, source_target_pairs={{0,2},{1,3},{2,0},{3,1},{4,6},{5,7},{6,4},{7,5},{8,10},{9,11},{10,... | collective-permute-start | bytes 688136 | tf_op jit(solution)/shard_map/ppermute | solution.py:199
  42.6 4.7 %collective-permute-start.3 = (f32[32,1792]{1,0:T(8,128)S(1)}, f32[32,1792]{1,0:T(8,128)S(1)}, u32[]{:S(2)}, u32[]{:S(2)}) collective-permute-start(f32[32,1792]{1,0:T(8,128)S(1)} %slice_add_fusion.2), channel_id=1, source_target_pairs={{4,0},{5,1},{6,2},{7,3},{12,8},{13,9},{14,10},{15,11},{16,20},{17,... | collective-permute-start | bytes 688136 | tf_op jit(solution)/shard_map/ppermute | solution.py:207
  48.0 12.2 %shard_map.51 = (f32[64,2048]{1,0:T(8,128)S(1)}, f32[64,2048]{1,0:T(8,128)S(1)}) custom-call(s32[512]{0:T(512)S(1)} %reshape.66.list_ref, s32[16]{0:T(128)S(1)} %and_select_fusion.count_ref, bf16[33,256,128]{2,1,0:T(8,128)(2,1)S(1)} %shard_map.50.l_ref, f32[4096,4096]{1,0:T(8,128)} %g_ref.11), custom_call_target="tpu_custom_call" | custom-call | flops 25769803776 | bytes 33554432 | tf_op jit(solution)/shard_map/pallas_call | solution.py:164
  60.4 1.3 %collective-permute-start.8 = (f32[32,1792]{1,0:T(8,128)S(1)}, f32[32,1792]{1,0:T(8,128)S(1)}, u32[]{:S(2)}, u32[]{:S(2)}) collective-permute-start(f32[32,1792]{1,0:T(8,128)S(1)} %slice_add_fusion.1), channel_id=1, source_target_pairs={{4,0},{5,1},{6,2},{7,3},{12,8},{13,9},{14,10},{15,11},{16,20},{17,... | collective-permute-start | bytes 688136 | tf_op jit(solution)/shard_map/ppermute | solution.py:207
  61.7 1.7 %collective-permute-start.12 = (f32[64,2048]{1,0:T(8,128)S(1)}, f32[64,2048]{1,0:T(8,128)S(1)}, u32[]{:S(2)}, u32[]{:S(2)}) collective-permute-start(f32[64,2048]{1,0:T(8,128)S(1)} %get-tuple-element.58), channel_id=1, source_target_pairs={{0,1},{1,0},{2,3},{3,2},{4,5},{5,4},{6,7},{7,6},{8,9},{9,8},{10,11... | collective-permute-start | bytes 1572872 | tf_op jit(solution)/shard_map/ppermute | solution.py:199
  63.7 7.8 %shard_map.52 = (f32[64,1280]{1,0:T(8,128)S(1)}, f32[64,1280]{1,0:T(8,128)S(1)}) custom-call(s32[512]{0:T(512)S(1)} %reshape.66.list_ref, s32[16]{0:T(128)S(1)} %and_select_fusion.count_ref, bf16[33,256,128]{2,1,0:T(8,128)(2,1)S(1)} %shard_map.50.l_ref, f32[4096,4096]{1,0:T(8,128)} %g_ref.11), custom_call_target="tpu_custom_call" | custom-call | flops 16106127360 | bytes 20971520 | tf_op jit(solution)/shard_map/pallas_call | solution.py:164
  72.3 3.0 %collective-permute-done.12 = f32[64,2048]{1,0:T(8,128)S(1)} collective-permute-done((f32[64,2048]{1,0:T(8,128)S(1)}, f32[64,2048]{1,0:T(8,128)S(1)}, u32[]{:S(2)}, u32[]{:S(2)}) %collective-permute-start.12) | collective-permute-done | bytes 524320 | tf_op jit(solution)/shard_map/ppermute | solution.py:199
  75.4 5.7 %shard_map.53 = (f32[64,768]{1,0:T(8,128)S(1)}, f32[64,768]{1,0:T(8,128)S(1)}) custom-call(s32[512]{0:T(512)S(1)} %reshape.66.list_ref, s32[16]{0:T(128)S(1)} %and_select_fusion.count_ref, bf16[33,256,128]{2,1,0:T(8,128)(2,1)S(1)} %shard_map.50.l_ref, f32[4096,4096]{1,0:T(8,128)} %g_ref.11), custom_call_target="tpu_custom_call" | custom-call | flops 9663676416 | bytes 12582912 | tf_op jit(solution)/shard_map/pallas_call | solution.py:164
  81.7 1.7 %collective-permute-start.13 = (f32[32,2048]{1,0:T(8,128)S(1)}, f32[32,2048]{1,0:T(8,128)S(1)}, u32[]{:S(2)}, u32[]{:S(2)}) collective-permute-start(f32[32,2048]{1,0:T(8,128)S(1)} %slice.67), channel_id=1, source_target_pairs={{0,2},{1,3},{2,0},{3,1},{4,6},{5,7},{6,4},{7,5},{8,10},{9,11},{10,... | collective-permute-start | bytes 786440 | tf_op jit(solution)/shard_map/ppermute | solution.py:199
  83.4 2.5 %collective-permute-start.18 = (f32[64,768]{1,0:T(8,128)S(1)}, f32[64,768]{1,0:T(8,128)S(1)}, u32[]{:S(2)}, u32[]{:S(2)}) collective-permute-start(f32[64,768]{1,0:T(8,128)S(1)} %get-tuple-element.66), channel_id=1, source_target_pairs={{0,1},{1,0},{2,3},{3,2},{4,5},{5,4},{6,7},{7,6},{8,9},{9,8},{10,11... | collective-permute-start | bytes 589832 | tf_op jit(solution)/shard_map/ppermute | solution.py:199
  85.9 2.5 %collective-permute-done.16 = f32[32,1280]{1,0:T(8,128)S(1)} collective-permute-done((f32[32,1280]{1,0:T(8,128)S(1)}, f32[32,1280]{1,0:T(8,128)S(1)}, u32[]{:S(2)}, u32[]{:S(2)}) %collective-permute-start.16) | collective-permute-done | bytes 163872 | tf_op jit(solution)/shard_map/ppermute | solution.py:199
  88.4 1.3 %collective-permute-start.17 = (f32[32,1280]{1,0:T(8,128)S(1)}, f32[32,1280]{1,0:T(8,128)S(1)}, u32[]{:S(2)}, u32[]{:S(2)}) collective-permute-start(f32[32,1280]{1,0:T(8,128)S(1)} %slice_add_fusion.3), channel_id=1, source_target_pairs={{0,4},{1,5},{2,6},{3,7},{8,12},{9,13},{10,14},{11,15},{20,16},{21,... | collective-permute-start | bytes 491528 | tf_op jit(solution)/shard_map/ppermute | solution.py:207
  90.3 4.3 %collective-permute-done.13 = f32[32,2048]{1,0:T(8,128)S(1)} collective-permute-done((f32[32,2048]{1,0:T(8,128)S(1)}, f32[32,2048]{1,0:T(8,128)S(1)}, u32[]{:S(2)}, u32[]{:S(2)}) %collective-permute-start.13) | collective-permute-done | bytes 262176 | tf_op jit(solution)/shard_map/ppermute | solution.py:199
  94.6 1.3 %collective-permute-start.14 = (f32[32,2048]{1,0:T(8,128)S(1)}, f32[32,2048]{1,0:T(8,128)S(1)}, u32[]{:S(2)}, u32[]{:S(2)}) collective-permute-start(f32[32,2048]{1,0:T(8,128)S(1)} %slice_add_fusion), channel_id=1, source_target_pairs={{0,4},{1,5},{2,6},{3,7},{8,12},{9,13},{10,14},{11,15},{20,16},{21,... | collective-permute-start | bytes 786440 | tf_op jit(solution)/shard_map/ppermute | solution.py:207
  97.2 6.9 %collective-permute-start.11 = (f32[32,512]{1,0:T(8,128)S(1)}, f32[32,512]{1,0:T(8,128)S(1)}, u32[]{:S(2)}, u32[]{:S(2)}) collective-permute-start(f32[32,512]{1,0:T(8,128)S(1)} %slice_add_fusion.5), channel_id=1, source_target_pairs={{4,0},{5,1},{6,2},{7,3},{12,8},{13,9},{14,10},{15,11},{16,20},{17,... | collective-permute-start | bytes 196616 | tf_op jit(solution)/shard_map/ppermute | solution.py:207
  104.1 1.9 %collective-permute-done.11 = f32[32,512]{1,0:T(8,128)S(1)} collective-permute-done((f32[32,512]{1,0:T(8,128)S(1)}, f32[32,512]{1,0:T(8,128)S(1)}, u32[]{:S(2)}, u32[]{:S(2)}) %collective-permute-start.11) | collective-permute-done | bytes 65568 | tf_op jit(solution)/shard_map/ppermute | solution.py:207
  106.0 1.5 %collective-permute-done.17 = f32[32,1280]{1,0:T(8,128)S(1)} collective-permute-done((f32[32,1280]{1,0:T(8,128)S(1)}, f32[32,1280]{1,0:T(8,128)S(1)}, u32[]{:S(2)}, u32[]{:S(2)}) %collective-permute-start.17) | collective-permute-done | bytes 163872 | tf_op jit(solution)/shard_map/ppermute | solution.py:207
  107.6 6.0 %collective-permute-done.20 = f32[32,768]{1,0:T(8,128)S(1)} collective-permute-done((f32[32,768]{1,0:T(8,128)S(1)}, f32[32,768]{1,0:T(8,128)S(1)}, u32[]{:S(2)}, u32[]{:S(2)}) %collective-permute-start.20) | collective-permute-done | bytes 98336 | tf_op jit(solution)/shard_map/ppermute | solution.py:207
  (70 shorter events, 11.2 us)
Async XLA Ops:
  0.0 2.9 %collective-permute-start = (f32[64,4096]{1,0:T(8,128)}, f32[64,4096]{1,0:T(8,128)S(1)}, u32[]{:S(2)}, u32[]{:S(2)}) collective-permute-start(f32[64,4096]{1,0:T(8,128)} %own_ref.1), channel_id=1, source_target_pairs={{0,8},{8,0},{16,24},{24,16},{1,9},{9,1},{17,25},{25,17},{2,10},{10... | collective-permute-start | bytes 3145736 | tf_op jit(solution)/shard_map/ppermute | solution.py:199
  0.0 31.1 %collective-permute-start.4 = (f32[64,4096]{1,0:T(8,128)}, f32[64,4096]{1,0:T(8,128)S(1)}, u32[]{:S(2)}, u32[]{:S(2)}) collective-permute-start(f32[64,4096]{1,0:T(8,128)} %own_ref.1), channel_id=1, source_target_pairs={{0,16},{8,24},{16,0},{24,8},{1,17},{9,25},{17,1},{25,9},{2,18},{10... | collective-permute-start | bytes 3145736 | tf_op jit(solution)/shard_map/ppermute | solution.py:199
  2.9 1.2 %copy-start = (f32[64,4096]{1,0:T(8,128)S(1)}, f32[64,4096]{1,0:T(8,128)}, u32[]{:S(2)}) copy-start(f32[64,4096]{1,0:T(8,128)} %own_ref.1) | copy-start | bytes 3145732
  15.8 12.7 %collective-permute-start.1 = (f32[64,1792]{1,0:T(8,128)S(1)}, f32[64,1792]{1,0:T(8,128)S(1)}, u32[]{:S(2)}, u32[]{:S(2)}) collective-permute-start(f32[64,1792]{1,0:T(8,128)S(1)} %get-tuple-element.37), channel_id=1, source_target_pairs={{0,1},{1,0},{2,3},{3,2},{4,5},{5,4},{6,7},{7,6},{8,9},{9,8},{10,11... | collective-permute-start | bytes 1376264 | tf_op jit(solution)/shard_map/ppermute | solution.py:199
  28.1 11.9 %collective-permute-start.6 = (f32[64,1792]{1,0:T(8,128)S(1)}, f32[64,1792]{1,0:T(8,128)S(1)}, u32[]{:S(2)}, u32[]{:S(2)}) collective-permute-start(f32[64,1792]{1,0:T(8,128)S(1)} %get-tuple-element.45), channel_id=1, source_target_pairs={{0,1},{1,0},{2,3},{3,2},{4,5},{5,4},{6,7},{7,6},{8,9},{9,8},{10,11... | collective-permute-start | bytes 1376264 | tf_op jit(solution)/shard_map/ppermute | solution.py:199
  28.6 14.0 %collective-permute-start.2 = (f32[32,1792]{1,0:T(8,128)S(1)}, f32[32,1792]{1,0:T(8,128)S(1)}, u32[]{:S(2)}, u32[]{:S(2)}) collective-permute-start(f32[32,1792]{1,0:T(8,128)S(1)} %slice.61), channel_id=1, source_target_pairs={{0,2},{1,3},{2,0},{3,1},{4,6},{5,7},{6,4},{7,5},{8,10},{9,11},{10,... | collective-permute-start | bytes 688136 | tf_op jit(solution)/shard_map/ppermute | solution.py:199
  31.1 16.1 %collective-permute-start.5 = (f32[64,4096]{1,0:T(8,128)S(1)}, f32[64,4096]{1,0:T(8,128)S(1)}, u32[]{:S(2)}, u32[]{:S(2)}) collective-permute-start(f32[64,4096]{1,0:T(8,128)S(1)} %collective-permute-done.4.own_ref), channel_id=1, source_target_pairs={{0,8},{8,0},{16,24},{24,16},{1,9},{9,1},{17,25},{25,17},{2,10},{10... | collective-permute-start | bytes 3145736 | tf_op jit(solution)/shard_map/ppermute | solution.py:199
  40.0 20.3 %collective-permute-start.7 = (f32[32,1792]{1,0:T(8,128)S(1)}, f32[32,1792]{1,0:T(8,128)S(1)}, u32[]{:S(2)}, u32[]{:S(2)}) collective-permute-start(f32[32,1792]{1,0:T(8,128)S(1)} %slice.63), channel_id=1, source_target_pairs={{0,2},{1,3},{2,0},{3,1},{4,6},{5,7},{6,4},{7,5},{8,10},{9,11},{10,... | collective-permute-start | bytes 688136 | tf_op jit(solution)/shard_map/ppermute | solution.py:199
  42.3 18.1 %collective-permute-start.9 = (f32[64,512]{1,0:T(8,128)S(1)}, f32[64,512]{1,0:T(8,128)S(1)}, u32[]{:S(2)}, u32[]{:S(2)}) collective-permute-start(f32[64,512]{1,0:T(8,128)S(1)} %get-tuple-element.52), channel_id=1, source_target_pairs={{0,1},{1,0},{2,3},{3,2},{4,5},{5,4},{6,7},{7,6},{8,9},{9,8},{10,11... | collective-permute-start | bytes 393224 | tf_op jit(solution)/shard_map/ppermute | solution.py:199
  42.6 17.8 %collective-permute-start.3 = (f32[32,1792]{1,0:T(8,128)S(1)}, f32[32,1792]{1,0:T(8,128)S(1)}, u32[]{:S(2)}, u32[]{:S(2)}) collective-permute-start(f32[32,1792]{1,0:T(8,128)S(1)} %slice_add_fusion.2), channel_id=1, source_target_pairs={{4,0},{5,1},{6,2},{7,3},{12,8},{13,9},{14,10},{15,11},{16,20},{17,... | collective-permute-start | bytes 688136 | tf_op jit(solution)/shard_map/ppermute | solution.py:207
  60.4 11.8 %collective-permute-start.8 = (f32[32,1792]{1,0:T(8,128)S(1)}, f32[32,1792]{1,0:T(8,128)S(1)}, u32[]{:S(2)}, u32[]{:S(2)}) collective-permute-start(f32[32,1792]{1,0:T(8,128)S(1)} %slice_add_fusion.1), channel_id=1, source_target_pairs={{4,0},{5,1},{6,2},{7,3},{12,8},{13,9},{14,10},{15,11},{16,20},{17,... | collective-permute-start | bytes 688136 | tf_op jit(solution)/shard_map/ppermute | solution.py:207
  61.7 13.6 %collective-permute-start.12 = (f32[64,2048]{1,0:T(8,128)S(1)}, f32[64,2048]{1,0:T(8,128)S(1)}, u32[]{:S(2)}, u32[]{:S(2)}) collective-permute-start(f32[64,2048]{1,0:T(8,128)S(1)} %get-tuple-element.58), channel_id=1, source_target_pairs={{0,1},{1,0},{2,3},{3,2},{4,5},{5,4},{6,7},{7,6},{8,9},{9,8},{10,11... | collective-permute-start | bytes 1572872 | tf_op jit(solution)/shard_map/ppermute | solution.py:199
  63.4 8.8 %collective-permute-start.10 = (f32[32,512]{1,0:T(8,128)S(1)}, f32[32,512]{1,0:T(8,128)S(1)}, u32[]{:S(2)}, u32[]{:S(2)}) collective-permute-start(f32[32,512]{1,0:T(8,128)S(1)} %slice.65), channel_id=1, source_target_pairs={{0,2},{1,3},{2,0},{3,1},{4,6},{5,7},{6,4},{7,5},{8,10},{9,11},{10,... | collective-permute-start | bytes 196616 | tf_op jit(solution)/shard_map/ppermute | solution.py:199
  71.5 9.6 %collective-permute-start.15 = (f32[64,1280]{1,0:T(8,128)S(1)}, f32[64,1280]{1,0:T(8,128)S(1)}, u32[]{:S(2)}, u32[]{:S(2)}) collective-permute-start(f32[64,1280]{1,0:T(8,128)S(1)} %get-tuple-element.64), channel_id=1, source_target_pairs={{0,1},{1,0},{2,3},{3,2},{4,5},{5,4},{6,7},{7,6},{8,9},{9,8},{10,11... | collective-permute-start | bytes 983048 | tf_op jit(solution)/shard_map/ppermute | solution.py:199
  81.2 7.2 %collective-permute-start.16 = (f32[32,1280]{1,0:T(8,128)S(1)}, f32[32,1280]{1,0:T(8,128)S(1)}, u32[]{:S(2)}, u32[]{:S(2)}) collective-permute-start(f32[32,1280]{1,0:T(8,128)S(1)} %slice.69), channel_id=1, source_target_pairs={{0,2},{1,3},{2,0},{3,1},{4,6},{5,7},{6,4},{7,5},{8,10},{9,11},{10,... | collective-permute-start | bytes 491528 | tf_op jit(solution)/shard_map/ppermute | solution.py:199
  81.7 31.9 %copy-start.1 = (f32[32,4096]{1,0:T(8,128)S(1)}, f32[32,4096]{1,0:T(8,128)}, u32[]{:S(2)}) copy-start(f32[32,4096]{1,0:T(8,128)} %param.7) | copy-start | bytes 1572868
  81.7 12.8 %collective-permute-start.13 = (f32[32,2048]{1,0:T(8,128)S(1)}, f32[32,2048]{1,0:T(8,128)S(1)}, u32[]{:S(2)}, u32[]{:S(2)}) collective-permute-start(f32[32,2048]{1,0:T(8,128)S(1)} %slice.67), channel_id=1, source_target_pairs={{0,2},{1,3},{2,0},{3,1},{4,6},{5,7},{6,4},{7,5},{8,10},{9,11},{10,... | collective-permute-start | bytes 786440 | tf_op jit(solution)/shard_map/ppermute | solution.py:199
  83.4 6.3 %collective-permute-start.18 = (f32[64,768]{1,0:T(8,128)S(1)}, f32[64,768]{1,0:T(8,128)S(1)}, u32[]{:S(2)}, u32[]{:S(2)}) collective-permute-start(f32[64,768]{1,0:T(8,128)S(1)} %get-tuple-element.66), channel_id=1, source_target_pairs={{0,1},{1,0},{2,3},{3,2},{4,5},{5,4},{6,7},{7,6},{8,9},{9,8},{10,11... | collective-permute-start | bytes 589832 | tf_op jit(solution)/shard_map/ppermute | solution.py:199
  88.4 19.1 %collective-permute-start.17 = (f32[32,1280]{1,0:T(8,128)S(1)}, f32[32,1280]{1,0:T(8,128)S(1)}, u32[]{:S(2)}, u32[]{:S(2)}) collective-permute-start(f32[32,1280]{1,0:T(8,128)S(1)} %slice_add_fusion.3), channel_id=1, source_target_pairs={{0,4},{1,5},{2,6},{3,7},{8,12},{9,13},{10,14},{11,15},{20,16},{21,... | collective-permute-start | bytes 491528 | tf_op jit(solution)/shard_map/ppermute | solution.py:207
  89.8 6.1 %collective-permute-start.19 = (f32[32,768]{1,0:T(8,128)S(1)}, f32[32,768]{1,0:T(8,128)S(1)}, u32[]{:S(2)}, u32[]{:S(2)}) collective-permute-start(f32[32,768]{1,0:T(8,128)S(1)} %slice.71), channel_id=1, source_target_pairs={{0,2},{1,3},{2,0},{3,1},{4,6},{5,7},{6,4},{7,5},{8,10},{9,11},{10,... | collective-permute-start | bytes 294920 | tf_op jit(solution)/shard_map/ppermute | solution.py:199
  94.6 19.0 %collective-permute-start.14 = (f32[32,2048]{1,0:T(8,128)S(1)}, f32[32,2048]{1,0:T(8,128)S(1)}, u32[]{:S(2)}, u32[]{:S(2)}) collective-permute-start(f32[32,2048]{1,0:T(8,128)S(1)} %slice_add_fusion), channel_id=1, source_target_pairs={{0,4},{1,5},{2,6},{3,7},{8,12},{9,13},{10,14},{11,15},{20,16},{21,... | collective-permute-start | bytes 786440 | tf_op jit(solution)/shard_map/ppermute | solution.py:207
  95.9 17.6 %collective-permute-start.20 = (f32[32,768]{1,0:T(8,128)S(1)}, f32[32,768]{1,0:T(8,128)S(1)}, u32[]{:S(2)}, u32[]{:S(2)}) collective-permute-start(f32[32,768]{1,0:T(8,128)S(1)} %slice_add_fusion.4), channel_id=1, source_target_pairs={{0,4},{1,5},{2,6},{3,7},{8,12},{9,13},{10,14},{11,15},{20,16},{21,... | collective-permute-start | bytes 294920 | tf_op jit(solution)/shard_map/ppermute | solution.py:207
  97.2 8.8 %collective-permute-start.11 = (f32[32,512]{1,0:T(8,128)S(1)}, f32[32,512]{1,0:T(8,128)S(1)}, u32[]{:S(2)}, u32[]{:S(2)}) collective-permute-start(f32[32,512]{1,0:T(8,128)S(1)} %slice_add_fusion.5), channel_id=1, source_target_pairs={{4,0},{5,1},{6,2},{7,3},{12,8},{13,9},{14,10},{15,11},{16,20},{17,... | collective-permute-start | bytes 196616 | tf_op jit(solution)/shard_map/ppermute | solution.py:207
